TPU v7x, 32 devices: a whole 2x2x4 slice. The times are simulated.
32 devices in a mesh: fsdp: 16 (over z, y, core), tp: 2 (over x).
Axes of the slice: x: 2, y: 2, z: 4, core: 2. Of those that a mesh axis runs over, the one named last changes fastest.
Arguments:
- tokens: bfloat16 [4096, 4096], P('fsdp', 'tp'), may hold values from -6 to 6
- w_feat: bfloat16 [3, 4096, 4096], P(None, 'fsdp', 'tp'), may hold values from -0.09375 to 0.09375
- short_filter: float32 [3, 256, 7], P(None, 'tp'), may hold values from -6 to 6
- long_filter: bfloat16 [256, 128], P('tp'), may hold values from -1.5 to 1.5
- doc_ids: int32 [4096], P('fsdp'), may hold values from 0 to 7, never falling along the last dimension, each value on 1 to 2048 neighbouring positions
- grad_out: bfloat16 [4096, 4096], P('fsdp', 'tp'), may hold values from -6 to 6
Outputs:
- mixed: bfloat16 [4096, 4096], P('fsdp', 'tp')
- input_grad: bfloat16 [4096, 4096], P('fsdp', 'tp')
Inputs may be any that keep to these rules, and one draw needn't show every extreme that they name: `doc_ids`: document numbers never fall along the positions; each document covers 1 to 2048 consecutive positions and one covers exactly 2048; every number from 0 to 7 occurs.
All inputs are finite; a program needn't handle non-finite values.
Results may differ from a plain program's by a relative error of at most 0.0081.
Values may be sent and summed in bfloat16 or wider, within the bound.
A program may use at most 192 MiB of HBM per device.

v0:
```python
import jax
import jax.numpy as jnp
from jax import lax
from jax.sharding import PartitionSpec as P


def shifted_2(value, axis, steps):
    count = lax.axis_size(axis)
    initial, last = (max(0, -steps), min(count, count - steps))
    return lax.ppermute(value, axis, [(source, source + steps) for source in range(initial, last)])


def causal_taps(extended, doc_ext, filters, lead_rows):
    row_count = extended.shape[0] - lead_rows
    doc_now = doc_ext[lead_rows:]
    bcast_shape = (row_count,) + (1,) * (extended.ndim - 1)
    summed = jnp.zeros((row_count,) + extended.shape[1:], jnp.float32)
    for offset in range(filters.shape[-1]):
        shifted = extended[lead_rows - offset : lead_rows - offset + row_count].astype(jnp.float32)
        same_doc = (
            (doc_ext[lead_rows - offset : lead_rows - offset + row_count] == doc_now)
            .astype(jnp.float32)
            .reshape(bcast_shape)
        )
        summed = summed + filters[..., offset] * shifted * same_doc
    return summed


def ahead_taps(extended, doc_ext, filters, row_count):
    doc_now = doc_ext[:row_count]
    bcast_shape = (row_count,) + (1,) * (extended.ndim - 1)
    summed = jnp.zeros((row_count,) + extended.shape[1:], jnp.float32)
    for offset in range(filters.shape[-1]):
        shifted = extended[offset : offset + row_count].astype(jnp.float32)
        same_doc = (
            (doc_ext[offset : offset + row_count] == doc_now)
            .astype(jnp.float32)
            .reshape(bcast_shape)
        )
        summed = summed + filters[..., offset] * shifted * same_doc
    return summed


def toeplitz_base(long_filter, anti_causal):
    tap_count = long_filter.shape[1]
    row_iota = lax.broadcasted_iota(jnp.int32, (tap_count, 2 * tap_count), 0)
    col_iota = lax.broadcasted_iota(jnp.int32, (tap_count, 2 * tap_count), 1)
    if anti_causal:
        lag_index = col_iota - row_iota
    else:
        lag_index = row_iota + tap_count - col_iota
    tap_iota = lax.broadcasted_iota(jnp.int32, (tap_count, tap_count, 2 * tap_count), 0)
    one_hot = (
        (tap_iota == lag_index[None])
        .astype(long_filter.dtype)
        .reshape(tap_count, 2 * tap_count * tap_count)
    )
    table = jnp.dot(long_filter, one_hot, preferred_element_type=jnp.float32).astype(
        long_filter.dtype
    )
    return table.reshape(long_filter.shape[0], tap_count, 2 * tap_count)


def blocked_conv(extended, doc_ext, toeplitz, doc_rows, row_count):
    groups = toeplitz.shape[0]
    tap_count = toeplitz.shape[1]
    chan_width = extended.shape[1]
    block_count = row_count // tap_count
    row_blocks = extended.reshape(block_count + 1, tap_count, chan_width)
    windows = jnp.concatenate([row_blocks[:-1], row_blocks[1:]], axis=1)
    doc_blocks = doc_ext.reshape(block_count + 1, tap_count)
    doc_windows = jnp.concatenate([doc_blocks[:-1], doc_blocks[1:]], axis=1)
    row_docs = doc_rows.reshape(block_count, tap_count)

    def one_block(inputs):
        window, col_docs, own_docs = inputs
        window = window.reshape(2 * tap_count, groups, chan_width // groups)
        kernel = toeplitz * (own_docs[:, None] == col_docs[None, :]).astype(toeplitz.dtype)[None]
        result = jnp.einsum("gtu,ugk->tgk", kernel, window, preferred_element_type=jnp.float32)
        return result.reshape(tap_count, chan_width)

    blocks = lax.map(one_block, (windows, doc_windows, row_docs))
    return blocks.reshape(row_count, chan_width)


def shards(tokens, w_feat, short_filter, long_filter, doc_ids, grad_out):
    rows_here = tokens.shape[0]
    tap_count = long_filter.shape[1]
    margin = 8
    reach_rows = tap_count + margin
    gathered = lax.all_gather(tokens, "tp", axis=1, tiled=True)
    filter_groups = short_filter.shape[1]
    short_full = jnp.broadcast_to(
        short_filter[:, :, None, :], (3, filter_groups, 16, short_filter.shape[2])
    ).reshape(3, filter_groups * 16, short_filter.shape[2])
    w_whole = lax.all_gather(w_feat, "fsdp", axis=1, tiled=True)
    u_all = jnp.einsum("sd,jdc->sjc", gathered, w_whole, preferred_element_type=jnp.float32).astype(
        jnp.bfloat16
    )
    u_pair = u_all[:, 1:]
    prev_pair, prev_doc = shifted_2(
        (u_pair[rows_here - reach_rows :], doc_ids[rows_here - reach_rows :]), "fsdp", 1
    )
    ext_pair = jnp.concatenate([prev_pair, u_pair], axis=0)
    ext_doc = jnp.concatenate([prev_doc, doc_ids], axis=0)
    conv_pair = causal_taps(ext_pair, ext_doc, short_full[1:], margin)
    product_kv = (conv_pair[:, 0] * conv_pair[:, 1]).astype(jnp.bfloat16)
    doc_product = ext_doc[margin:]
    long_out = blocked_conv(
        product_kv, doc_product, toeplitz_base(long_filter, False), doc_ids, rows_here
    )
    conv_pair, long_out, prev_doc = (
        conv_pair[tap_count:],
        long_out,
        prev_doc[reach_rows - margin :],
    )
    u_query = u_all[:, 0]
    prev_query = shifted_2(u_query[rows_here - margin :], "fsdp", 1)
    ext_query = jnp.concatenate([prev_query, u_query], axis=0)
    ext_doc = jnp.concatenate([prev_doc, doc_ids], axis=0)
    conv_query = causal_taps(ext_query, ext_doc, short_full[0], margin)
    pieces = ((0, 3, w_whole),)
    block_out = (conv_query * long_out).astype(jnp.bfloat16)
    grad_float = grad_out.astype(jnp.float32)
    grad_long = (grad_float * conv_query).astype(jnp.bfloat16)
    grad_query = grad_float * long_out
    next_grad, next_doc = shifted_2((grad_long[:tap_count], doc_ids[:tap_count]), "fsdp", -1)
    ext_grad = jnp.concatenate([grad_long, next_grad], axis=0)
    ext_doc = jnp.concatenate([doc_ids, next_doc], axis=0)
    grad_mixed = blocked_conv(
        ext_grad, ext_doc, toeplitz_base(long_filter, True), doc_ids, rows_here
    )
    grad_feat = jnp.stack(
        [grad_query, grad_mixed * conv_pair[:, 1], grad_mixed * conv_pair[:, 0]], axis=1
    ).astype(jnp.bfloat16)
    next_feat = shifted_2(grad_feat[:margin], "fsdp", -1)
    ext_feat = jnp.concatenate([grad_feat, next_feat], axis=0)
    doc_feat = jnp.concatenate([doc_ids, next_doc[:margin]], axis=0)
    grad_u = ahead_taps(ext_feat, doc_feat, short_full, rows_here).astype(jnp.bfloat16)
    first_role, end_role, weights = pieces[0]
    partial_value = jnp.einsum("sjc,jdc->sd", grad_u, weights, preferred_element_type=jnp.float32)
    input_grad = lax.psum_scatter(
        partial_value.astype(jnp.bfloat16), "tp", scatter_dimension=1, tiled=True
    )
    return (block_out, input_grad)


def solution(mesh):
    in_specs = (
        P("fsdp", "tp"),
        P(None, "fsdp", "tp"),
        P(None, "tp", None),
        P("tp", None),
        P("fsdp"),
        P("fsdp", "tp"),
    )
    out_specs = (P("fsdp", "tp"), P("fsdp", "tp"))
    return jax.shard_map(shards, mesh=mesh, in_specs=in_specs, out_specs=out_specs, check_vma=False)
```

profile of v0, /device:TPU:0, one launch (start us, length us, event | category | flops | bytes accessed | tf_op | source)
XLA Modules:
  0.0 490.7 jit_solution(5397390255139693855)
XLA Ops:
  8.8 2.3 collective-permute-start.1
  15.6 4.7 convolution_convert_fusion
  20.4 4.6 convolution_convert_fusion.1
  25.0 12.7 %copy.35 = bf16[128,128,256]{2,1,0:T(8,128)(2,1)} copy(bf16[128,128,256]{0,2,1:T(8,128)(2,1)} %bitcast.135) | data formatting | bytes 16777216 | tf_op jit(solution)/shard_map/while | solution.py:82
  37.7 12.7 %copy.31 = bf16[128,128,256]{2,1,0:T(8,128)(2,1)} copy(bf16[128,128,256]{0,2,1:T(8,128)(2,1)} %bitcast.136) | data formatting | bytes 16777216 | tf_op jit(solution)/shard_map/while | solution.py:82
  50.7 243.4 %all-gather.5.cloned.1.call-done = bf16[3,4096,2048]{2,1,0:T(8,128)(2,1)} async-done(((bf16[3,256,2048]{2,1,0:T(8,128)(2,1)}), bf16[3,4096,2048]{2,1,0:T(8,128)(2,1)}) %all-gather.5.cloned.1.call-update) | async-done | bytes 50331664 | tf_op jit(solution)/shard_map/all_gather | solution.py:96
  294.1 21.2 %convolution_convert_fusion.2 = bf16[256,3,2048]{2,0,1:T(8,128)(2,1)S(1)} fusion(bf16[3,4096,2048]{2,1,0:T(8,128)(2,1)} %all-gather.5.cloned.1.call-done, bf16[256,4096]{1,0:T(8,128)(2,1)} %all-gather.3.cloned.1.call-done), kind=kOutput, calls=%fused_computation.42 | convolution fusion | flops 12886474752 | bytes 55574528 | tf_op jit(solution)/shard_map/sd,jdc->sjc/dot_general | solution.py:97
  315.4 2.2 collective-permute-start
  318.4 4.0 fusion.42
  322.4 1.5 collective-permute-start.3
  325.1 1.5 slice.413
  326.6 4.5 collective-permute-start.2
  333.5 1.6 pad_maximum_fusion.4
  335.1 1.6 broadcast.89.clone2.1
  336.7 17.0 %while.21 = (s32[]{:T(128)}, f32[2,128,2048]{2,1,0:T(8,128)}, bf16[2,256,2048]{1,2,0:T(8,128)(2,1)}, s32[2,128]{1,0:T(2,128)S(1)}, s32[2,256]{1,0:T(2,128)S(1)}, /*index=5*/bf16[128,128,256]{2,1,0:T(8,128)(2,1)}, s32[]{:T(128)}) while((s32[]{:T(128)}, f32[2,128,2048]{2,1,0:T(8,128)}, bf16[2,256,2048]{1,2,0:T(8,128)(2,1)}, ...), condition=%wide.region_3.4_spmd, body=%wide.region_2.3_spmd.sunk | while | flops 138477568 | bytes 16913496 | solution.py:82
  338.1 5.7 %fusion.83 = f32[128,16,128]{2,1,0:T(8,128)S(1)} fusion(bf16[256,128,16]{0,2,1:T(8,128)(2,1)S(1)} %bitcast.131, bf16[128,128,256]{2,1,0:T(8,128)(2,1)} %get-tuple-element.307, bf16[128,256]{1,0:T(8,128)(2,1)S(1)} %compare_convert_fusion.17), kind=kOutput, calls=%fused_computation.9.clone.1 | convolution fusion | flops 138412032 | bytes 10551296 | tf_op jit(solution)/shard_map/while/body/eval_jaxpr/gtu,ugk->tgk/dot_general | solution.py:79
  346.6 5.7 %fusion.83 = f32[128,16,128]{2,1,0:T(8,128)S(1)} fusion(bf16[256,128,16]{0,2,1:T(8,128)(2,1)S(1)} %bitcast.131, bf16[128,128,256]{2,1,0:T(8,128)(2,1)} %get-tuple-element.307, bf16[128,256]{1,0:T(8,128)(2,1)S(1)} %compare_convert_fusion.17), kind=kOutput, calls=%fused_computation.9.clone.1 | convolution fusion | flops 138412032 | bytes 10551296 | tf_op jit(solution)/shard_map/while/body/eval_jaxpr/gtu,ugk->tgk/dot_general | solution.py:79
  353.8 20.9 %multiply_add_fusion = f32[384,2,2048]{2,0,1:T(8,128)S(1)} fusion(bf16[256,2,2048]{2,0,1:T(8,128)(2,1)} %slice.413, bf16[136,2,2048]{2,0,1:T(8,128)(2,1)} %collective-permute-done.2, f32[384]{0:T(512)S(1)} %get-tuple-element.172, f32[2,2048]{1,0:T(2,128)S(1)} %get-tuple-element.146, f32[384]{0:T(512)S(1)} %get-tuple-element.173, ...), kind=kLoop, calls=%fused_computation.33 | loop fusion | flops 73924608 | bytes 9626624 | tf_op jit(solution)/shard_map/add | solution.py:25
  376.3 1.7 fusion.44
  379.2 1.6 copy.29
  380.8 1.3 copy.30
  382.1 2.8 pad_maximum_fusion.3
  385.0 1.6 broadcast.89.clone2
  386.5 17.0 %while.20 = (s32[]{:T(128)}, f32[2,128,2048]{2,1,0:T(8,128)}, bf16[2,256,2048]{1,2,0:T(8,128)(2,1)}, s32[2,128]{1,0:T(2,128)S(1)}, s32[2,256]{1,0:T(2,128)S(1)}, /*index=5*/bf16[128,128,256]{2,1,0:T(8,128)(2,1)}, s32[]{:T(128)}) while((s32[]{:T(128)}, f32[2,128,2048]{2,1,0:T(8,128)}, bf16[2,256,2048]{1,2,0:T(8,128)(2,1)}, ...), condition=%wide.region_1.2_spmd, body=%wide.region_0.1_spmd.sunk | while | flops 138477568 | bytes 16913496 | solution.py:82
  386.6 1.3 constant_dynamic-slice_fusion.10
  388.0 5.7 %fusion.79 = f32[128,16,128]{2,1,0:T(8,128)S(1)} fusion(bf16[256,128,16]{0,2,1:T(8,128)(2,1)S(1)} %bitcast.132, bf16[128,128,256]{2,1,0:T(8,128)(2,1)} %get-tuple-element.286, bf16[128,256]{1,0:T(8,128)(2,1)S(1)} %compare_convert_fusion.16), kind=kOutput, calls=%fused_computation.clone.1 | convolution fusion | flops 138412032 | bytes 10551296 | tf_op jit(solution)/shard_map/while/body/eval_jaxpr/gtu,ugk->tgk/dot_general | solution.py:79
  396.4 5.7 %fusion.79 = f32[128,16,128]{2,1,0:T(8,128)S(1)} fusion(bf16[256,128,16]{0,2,1:T(8,128)(2,1)S(1)} %bitcast.132, bf16[128,128,256]{2,1,0:T(8,128)(2,1)} %get-tuple-element.286, bf16[128,256]{1,0:T(8,128)(2,1)S(1)} %compare_convert_fusion.16), kind=kOutput, calls=%fused_computation.clone.1 | convolution fusion | flops 138412032 | bytes 10551296 | tf_op jit(solution)/shard_map/while/body/eval_jaxpr/gtu,ugk->tgk/dot_general | solution.py:79
  403.5 4.2 fusion.41
  409.4 4.1 collective-permute-done.5
  413.5 1.9 pad_maximum_fusion
  415.4 31.4 %fusion.14 = bf16[256,4096]{1,0:T(8,128)(2,1)} fusion(bf16[3,4096,2048]{2,1,0:T(8,128)(2,1)} %all-gather.5.cloned.1.call-done, bf16[264,3,2048]{2,0,1:T(8,128)(2,1)} %pad_maximum_fusion, f32[256]{0:T(256)S(1)} %get-tuple-element.163, f32[3,2048]{1,0:T(4,128)S(1)} %get-tuple-element.187, f32[256]{0:T(256)S(1)} %get-tuple-element.164, ...), kind=kOutput, calls=%fused_computation.35 | convolution fusion | flops 12931563520 | bytes 74627072 | tf_op jit(solution)/shard_map/sjc,jdc->sd/dot_general | solution.py:141
  446.8 37.3 %reduce-scatter.2.cloned.1.call-done = bf16[256,2048]{1,0:T(8,128)(2,1)} async-done(((bf16[256,4096]{1,0:T(8,128)(2,1)}), bf16[256,2048]{1,0:T(8,128)(2,1)}) %reduce-scatter.2.cloned.1.call-update) | async-done | bytes 1048592 | tf_op jit(solution)/shard_map/reduce_scatter | solution.py:142
  (97 shorter events, 25.2 us)
Async XLA Ops:
  7.2 8.5 %copy-start = (bf16[128,128]{1,0:T(8,128)(2,1)S(1)}, bf16[128,128]{1,0:T(8,128)(2,1)}, u32[]{:S(2)}) copy-start(bf16[128,128]{1,0:T(8,128)(2,1)} %param.13) | copy-start | bytes 98308
  7.2 1.6 copy-start.6
  7.2 5.3 %copy-start.5 = (f32[3,128,7]{1,2,0:T(8,128)S(1)}, f32[3,128,7]{1,2,0:T(8,128)}, u32[]{:S(2)}) copy-start(f32[3,128,7]{1,2,0:T(8,128)} %param.12) | copy-start | bytes 32260
  7.2 5.9 %slice-start = ((f32[3,128,7]{1,2,0:T(8,128)}), f32[2,128,7]{1,2,0:T(8,128)S(1)}, s32[]{:S(2)}) async-start(f32[3,128,7]{1,2,0:T(8,128)} %param.12), calls=%async_computation.4 | async-start | bytes 16384 | tf_op jit(solution)/shard_map/slice | solution.py:106
  7.2 43.5 %all-gather.3.cloned.1.call-start = ((), (), s32[]{:S(2)}) async-start(), calls=%async_computation.1 | async-start | bytes 3145728 | tf_op jit(solution)/shard_map/all_gather | solution.py:91
  7.9 286.2 %all-gather.5.cloned.1.call-start = ((), (), s32[]{:S(2)}) async-start(), calls=%async_computation.2 | async-start | bytes 53477376 | tf_op jit(solution)/shard_map/all_gather | solution.py:96
  8.7 475.5 %reduce-scatter.2.cloned.1.call-start = ((), (), s32[]{:S(2)}) async-start(), calls=%async_computation.3 | async-start | bytes 3145728 | tf_op jit(solution)/shard_map/reduce_scatter | solution.py:142
  8.8 41.5 %collective-permute-start.1 = (s32[136]{0:T(256)S(1)}, s32[136]{0:T(256)S(1)}, u32[]{:S(2)}, u32[]{:S(2)}) collective-permute-start(s32[136]{0:T(256)S(1)} %slice.310), channel_id=1, source_target_pairs={{0,2},{2,4},{4,6},{6,8},{8,10},{10,12},{12,14},{14,16},{16,18},{18... | collective-permute-start | bytes 1640 | tf_op jit(solution)/shard_map/ppermute | solution.py:10
  11.2 39.2 %collective-permute-start.4 = (s32[128]{0:T(128)S(1)}, s32[128]{0:T(128)S(1)}, u32[]{:S(2)}, u32[]{:S(2)}) collective-permute-start(s32[128]{0:T(128)S(1)} %slice.367), channel_id=1, source_target_pairs={{2,0},{4,2},{6,4},{8,6},{10,8},{12,10},{14,12},{16,14},{18,16},{20... | collective-permute-start | bytes 1544 | tf_op jit(solution)/shard_map/ppermute | solution.py:10
  50.6 267.7 %copy-start.4 = (bf16[256,2048]{1,0:T(8,128)(2,1)S(1)}, bf16[256,2048]{1,0:T(8,128)(2,1)}, u32[]{:S(2)}) copy-start(bf16[256,2048]{1,0:T(8,128)(2,1)} %param.15) | copy-start | bytes 3145732
  315.4 3.0 collective-permute-start
  322.4 9.4 %collective-permute-start.3 = (bf16[128,2048]{1,0:T(8,128)(2,1)S(1)}, bf16[128,2048]{1,0:T(8,128)(2,1)}, u32[]{:S(2)}, u32[]{:S(2)}) collective-permute-start(bf16[128,2048]{1,0:T(8,128)(2,1)S(1)} %slice.437), channel_id=1, source_target_pairs={{2,0},{4,2},{6,4},{8,6},{10,8},{12,10},{14,12},{16,14},{18,16},{20... | collective-permute-start | bytes 1572872 | tf_op jit(solution)/shard_map/ppermute | solution.py:10
  326.6 27.2 %collective-permute-start.2 = (bf16[136,2,2048]{2,0,1:T(8,128)(2,1)}, bf16[136,2,2048]{2,0,1:T(8,128)(2,1)}, u32[]{:S(2)}, u32[]{:S(2)}) collective-permute-start(bf16[136,2,2048]{2,0,1:T(8,128)(2,1)} %slice.412), channel_id=1, source_target_pairs={{0,2},{2,4},{4,6},{6,8},{8,10},{10,12},{12,14},{14,16},{16,18},{18... | collective-permute-start | bytes 3342344 | tf_op jit(solution)/shard_map/ppermute | solution.py:10
  374.7 1.6 copy-start.3
  403.5 4.2 copy-start.2
  408.0 5.5 %collective-permute-start.5 = (bf16[8,3,2048]{2,0,1:T(8,128)(2,1)S(1)}, bf16[8,3,2048]{2,0,1:T(8,128)(2,1)S(1)}, u32[]{:S(2)}, u32[]{:S(2)}) collective-permute-start(bf16[8,3,2048]{2,0,1:T(8,128)(2,1)S(1)} %slice.441), channel_id=1, source_target_pairs={{2,0},{4,2},{6,4},{8,6},{10,8},{12,10},{14,12},{16,14},{18,16},{20... | collective-permute-start | bytes 294920 | tf_op jit(solution)/shard_map/ppermute | solution.py:10
  415.4 68.7 %copy-start.1 = (bf16[128,128]{1,0:T(8,128)(2,1)S(1)}, bf16[128,128]{1,0:T(8,128)(2,1)}, u32[]{:S(2)}) copy-start(bf16[128,128]{1,0:T(8,128)(2,1)} %param.13) | copy-start | bytes 98308
Sparse Core Ops, SparseCore 0:
  9.6 35.8 all-gather.2
  47.0 247.0 all-gather.4
  446.9 37.1 reduce-scatter.1
where the time goes:
time: 492 us; the launch traced here: 491 us
  waiting for transfers between devices  287 us (58%)
  matrix products  84.6 us (17%)
  local copies, waits for them, and re-layouts  52.1 us (11%)
  other arithmetic  39.6 us (8%)
  between operations  14.1 us (3%)
  starting transfers between devices  13.2 us (3%)
    all_gather x1, waiting for transfers between devices, shards(): w_whole = lax.all_gather(w_feat, 'fsdp', axis=1, tiled=True)  243 us
    reduce_scatter x1, waiting for transfers between devices, shards(): lax.psum_scatter(partial_value.astype(jnp.bfloat16), 'tp', scatter_dimens...  37.3 us
    dot_general x1, matrix products, shards(): jnp.einsum('sjc,jdc->sd', grad_u, weights, preferred_element_type=jnp.flo...  31.4 us
    while x2, local copies, waits for them, and re-layouts, blocked_conv(): blocks = lax.map(one_block, (windows, doc_windows, row_docs))  25.4 us
    dot_general x4, matrix products, one_block(): jnp.einsum('gtu,ugk->tgk', kernel, window, preferred_element_type=jnp.flo...  22.6 us
    dot_general x1, matrix products, shards(): jnp.einsum('sd,jdc->sjc', gathered, w_whole, preferred_element_type=jnp.f...  21.2 us
    add x1, other arithmetic, causal_taps(): summed = summed + filters[..., offset] * shifted * same_doc  20.9 us
    ppermute x6, starting transfers between devices, shifted_2(): lax.ppermute(value, axis, [(source, source + steps) for source in range(i...  13.1 us
  transfers between devices with their start and end apart: 9, of which 4 were waited for; matrix products, arithmetic and copies ran while one was open for 13% of the time, Pallas kernels for 0%

commit v1 on v0

--- a/solution.py
+++ b/solution.py
@@ -93,7 +93,23 @@
     short_full = jnp.broadcast_to(
         short_filter[:, :, None, :], (3, filter_groups, 16, short_filter.shape[2])
     ).reshape(3, filter_groups * 16, short_filter.shape[2])
-    w_whole = lax.all_gather(w_feat, "fsdp", axis=1, tiled=True)
+    ways, here, turn = (lax.axis_size("fsdp"), lax.axis_index("fsdp"), w_feat.shape[1])
+    shape = [n * ways if d == 1 else n for d, n in enumerate(w_feat.shape)]
+    full = lax.dynamic_update_slice_in_dim(
+        jnp.zeros(shape, w_feat.dtype), w_feat, here * turn, axis=1
+    )
+    going_up = going_down = w_feat
+    for far in range(1, ways // 2 + 1):
+        going_up = lax.ppermute(going_up, "fsdp", [(d, (d + 1) % ways) for d in range(ways)])
+        full = lax.dynamic_update_slice_in_dim(full, going_up, (here - far) % ways * turn, axis=1)
+        if 2 * far < ways:
+            going_down = lax.ppermute(
+                going_down, "fsdp", [(d, (d - 1) % ways) for d in range(ways)]
+            )
+            full = lax.dynamic_update_slice_in_dim(
+                full, going_down, (here + far) % ways * turn, axis=1
+            )
+    w_whole = full
     u_all = jnp.einsum("sd,jdc->sjc", gathered, w_whole, preferred_element_type=jnp.float32).astype(
         jnp.bfloat16
     )

time: 492 us -> 769 us (1.56)
  starting transfers between devices: 13.2 us -> 394 us
  waiting for transfers between devices: 287 us -> 103 us
  local copies, waits for them, and re-layouts: 52.1 us -> 128 us
    ppermute x0 -> x15, starting transfers between devices: none -> 349 us  [the longest x8 341 us: shards(): lax.ppermute(going_up, 'fsdp', [(d, (d + 1) % ways) for d in range(ways)])]
    all_gather x1 -> x0, waiting for transfers between devices: 243 us -> none  [shards(): w_whole = lax.all_gather(w_feat, 'fsdp', axis=1, tiled=True)]
    ppermute x0 -> x15, waiting for transfers between devices: none -> 53.2 us  [the longest x8 53.2 us: shards(): lax.ppermute(going_up, 'fsdp', [(d, (d + 1) % ways) for d in range(ways)])]
    dynamic_update_slice x0 -> x16, local copies, waits for them, and re-layouts: none -> 51 us  [the longest x8 26.4 us: shards(): lax.dynamic_update_slice_in_dim(full, going_up, (here - far) % ways * tur...]
    ppermute x6, starting transfers between devices: 13.1 us -> 45.6 us  [shifted_2(): lax.ppermute(value, axis, [(source, source + steps) for source in range(i...]
    broadcast_in_dim x0 -> x1, local copies, waits for them, and re-layouts: none -> 16.1 us  [shards(): jnp.zeros(shape, w_feat.dtype)]
    reduce_scatter x1, waiting for transfers between devices: 37.3 us -> 45.5 us  [shards(): lax.psum_scatter(partial_value.astype(jnp.bfloat16), 'tp', scatter_dimens...]
  transfers between devices with their start and end apart: 9 -> 23, of which waited for: 4 -> 7; matrix products, arithmetic and copies ran while one was open for 13% -> 18% of each run, Pallas kernels for 0% -> 0%
where the time goes in v1:
time: 769 us; the launch traced here: 767 us
  starting transfers between devices  394 us (51%)
  local copies, waits for them, and re-layouts  128 us (17%)
  waiting for transfers between devices  103 us (13%)
  matrix products  84.5 us (11%)
  other arithmetic  42.6 us (6%)
  between operations  14.6 us (2%)
    ppermute x8, starting transfers between devices, shards(): lax.ppermute(going_up, 'fsdp', [(d, (d + 1) % ways) for d in range(ways)])  341 us
    ppermute x8, waiting for transfers between devices, shards(): lax.ppermute(going_up, 'fsdp', [(d, (d + 1) % ways) for d in range(ways)])  53.2 us
    ppermute x6, starting transfers between devices, shifted_2(): lax.ppermute(value, axis, [(source, source + steps) for source in range(i...  45.6 us
    reduce_scatter x1, waiting for transfers between devices, shards(): lax.psum_scatter(partial_value.astype(jnp.bfloat16), 'tp', scatter_dimens...  45.5 us
    dot_general x1, matrix products, shards(): jnp.einsum('sjc,jdc->sd', grad_u, weights, preferred_element_type=jnp.flo...  31.3 us
    dynamic_update_slice x8, local copies, waits for them, and re-layouts, shards(): lax.dynamic_update_slice_in_dim(full, going_up, (here - far) % ways * tur...  26.4 us
    while x2, local copies, waits for them, and re-layouts, blocked_conv(): blocks = lax.map(one_block, (windows, doc_windows, row_docs))  25.3 us
    dot_general x4, matrix products, one_block(): jnp.einsum('gtu,ugk->tgk', kernel, window, preferred_element_type=jnp.flo...  22.6 us
  transfers between devices with their start and end apart: 23, of which 7 were waited for; matrix products, arithmetic and copies ran while one was open for 18% of the time, Pallas kernels for 0%

profile of v1, /device:TPU:0, one launch (start us, length us, event | category | flops | bytes accessed | tf_op | source)
XLA Modules:
  0.0 767.2 jit_solution(8759346036366072058)
XLA Ops:
  7.7 5.1 collective-permute-start.1
  12.8 35.2 %collective-permute-done = bf16[3,256,2048]{2,1,0:T(8,128)(2,1)S(1)} collective-permute-done((bf16[3,256,2048]{2,1,0:T(8,128)(2,1)}, bf16[3,256,2048]{2,1,0:T(8,128)(2,1)S(1)}, u32[]{:S(2)}, u32[]{:S(2)}) %collective-permute-start) | collective-permute-done | bytes 3145760 | tf_op jit(solution)/shard_map/ppermute | solution.py:103
  48.0 30.6 %collective-permute-start.2 = (bf16[3,256,2048]{2,1,0:T(8,128)(2,1)S(1)}, bf16[3,256,2048]{2,1,0:T(8,128)(2,1)S(1)}, u32[]{:S(2)}, u32[]{:S(2)}) collective-permute-start(bf16[3,256,2048]{2,1,0:T(8,128)(2,1)S(1)} %collective-permute-done), channel_id=1, source_target_pairs={{0,2},{2,4},{4,6},{6,8},{8,10},{10,12},{12,14},{14,16},{16,18},{18... | collective-permute-start | bytes 9437192 | tf_op jit(solution)/shard_map/ppermute | solution.py:103
  78.6 8.9 %collective-permute-done.2 = bf16[3,256,2048]{2,1,0:T(8,128)(2,1)S(1)} collective-permute-done((bf16[3,256,2048]{2,1,0:T(8,128)(2,1)S(1)}, bf16[3,256,2048]{2,1,0:T(8,128)(2,1)S(1)}, u32[]{:S(2)}, u32[]{:S(2)}) %collective-permute-start.2) | collective-permute-done | bytes 3145760 | tf_op jit(solution)/shard_map/ppermute | solution.py:103
  87.5 60.7 %collective-permute-start.4 = (bf16[3,256,2048]{2,1,0:T(8,128)(2,1)S(1)}, bf16[3,256,2048]{2,1,0:T(8,128)(2,1)S(1)}, u32[]{:S(2)}, u32[]{:S(2)}) collective-permute-start(bf16[3,256,2048]{2,1,0:T(8,128)(2,1)S(1)} %collective-permute-done.2), channel_id=1, source_target_pairs={{0,2},{2,4},{4,6},{6,8},{8,10},{10,12},{12,14},{14,16},{16,18},{18... | collective-permute-start | bytes 9437192 | tf_op jit(solution)/shard_map/ppermute | solution.py:103
  153.5 65.1 %collective-permute-start.6 = (bf16[3,256,2048]{2,1,0:T(8,128)(2,1)S(1)}, bf16[3,256,2048]{2,1,0:T(8,128)(2,1)}, u32[]{:S(2)}, u32[]{:S(2)}) collective-permute-start(bf16[3,256,2048]{2,1,0:T(8,128)(2,1)S(1)} %collective-permute-done.4), channel_id=1, source_target_pairs={{0,2},{2,4},{4,6},{6,8},{8,10},{10,12},{12,14},{14,16},{16,18},{18... | collective-permute-start | bytes 9437192 | tf_op jit(solution)/shard_map/ppermute | solution.py:103
  218.7 5.4 collective-permute-done.6
  224.1 64.4 %collective-permute-start.8 = (bf16[3,256,2048]{2,1,0:T(8,128)(2,1)}, bf16[3,256,2048]{2,1,0:T(8,128)(2,1)}, u32[]{:S(2)}, u32[]{:S(2)}) collective-permute-start(bf16[3,256,2048]{2,1,0:T(8,128)(2,1)} %collective-permute-done.6), channel_id=1, source_target_pairs={{0,2},{2,4},{4,6},{6,8},{8,10},{10,12},{12,14},{14,16},{16,18},{18... | collective-permute-start | bytes 9437192 | tf_op jit(solution)/shard_map/ppermute | solution.py:103
  289.9 5.0 collective-permute-start.16
  302.0 57.3 %collective-permute-start.10 = (bf16[3,256,2048]{2,1,0:T(8,128)(2,1)}, bf16[3,256,2048]{2,1,0:T(8,128)(2,1)}, u32[]{:S(2)}, u32[]{:S(2)}) collective-permute-start(bf16[3,256,2048]{2,1,0:T(8,128)(2,1)} %collective-permute-done.8), channel_id=1, source_target_pairs={{0,2},{2,4},{4,6},{6,8},{8,10},{10,12},{12,14},{14,16},{16,18},{18... | collective-permute-start | bytes 9437192 | tf_op jit(solution)/shard_map/ppermute | solution.py:103
  360.2 4.6 convolution_convert_fusion
  364.8 4.6 convolution_convert_fusion.1
  370.1 60.0 %collective-permute-start.12 = (bf16[3,256,2048]{2,1,0:T(8,128)(2,1)}, bf16[3,256,2048]{2,1,0:T(8,128)(2,1)}, u32[]{:S(2)}, u32[]{:S(2)}) collective-permute-start(bf16[3,256,2048]{2,1,0:T(8,128)(2,1)} %collective-permute-done.10), channel_id=1, source_target_pairs={{0,2},{2,4},{4,6},{6,8},{8,10},{10,12},{12,14},{14,16},{16,18},{18... | collective-permute-start | bytes 9437192 | tf_op jit(solution)/shard_map/ppermute | solution.py:103
  430.0 16.1 %broadcast_in_dim.32 = bf16[3,4096,2048]{2,1,0:T(8,128)(2,1)} broadcast(bf16[]{:T(256)} %constant.116.clone.1), dimensions={} | broadcast | bytes 50331648 | tf_op jit(solution)/shard_map/broadcast_in_dim | solution.py:99
  448.1 12.5 %copy.35 = bf16[128,128,256]{2,1,0:T(8,128)(2,1)} copy(bf16[128,128,256]{0,2,1:T(8,128)(2,1)} %bitcast.137) | data formatting | bytes 16777216 | tf_op jit(solution)/shard_map/while | solution.py:82
  460.6 12.8 %copy.31 = bf16[128,128,256]{2,1,0:T(8,128)(2,1)} copy(bf16[128,128,256]{0,2,1:T(8,128)(2,1)} %bitcast.138) | data formatting | bytes 16777216 | tf_op jit(solution)/shard_map/while | solution.py:82
  503.0 4.0 constant_dynamic-update-slice_fusion.9
  507.1 4.1 constant_dynamic-update-slice_fusion.8
  511.2 4.1 constant_dynamic-update-slice_fusion.7
  531.7 21.3 %fusion.41 = bf16[256,3,2048]{2,0,1:T(8,128)(2,1)S(1)} fusion(bf16[3,4096,2048]{2,1,0:T(8,128)(2,1)} %constant_dynamic-update-slice_fusion.2, bf16[256,4096]{1,0:T(8,128)(2,1)} %all-gather.2.cloned.1.call-done), kind=kOutput, calls=%fused_computation.73 | convolution fusion | flops 12886474752 | bytes 55574528 | tf_op jit(solution)/shard_map/sd,jdc->sjc/dot_general | solution.py:113
  553.1 32.7 %collective-permute-start.15 = (bf16[8,2048]{1,0:T(8,128)(2,1)S(1)}, bf16[8,2048]{1,0:T(8,128)(2,1)S(1)}, u32[]{:S(2)}, u32[]{:S(2)}) collective-permute-start(bf16[8,2048]{1,0:T(8,128)(2,1)S(1)} %slice_bitcast_fusion.1), channel_id=1, source_target_pairs={{0,2},{2,4},{4,6},{6,8},{8,10},{10,12},{12,14},{14,16},{16,18},{18... | collective-permute-start | bytes 98312 | tf_op jit(solution)/shard_map/ppermute | solution.py:10
  594.7 4.0 collective-permute-start.17
  604.4 17.1 %while.21 = (s32[]{:T(128)}, f32[2,128,2048]{2,1,0:T(8,128)}, bf16[2,256,2048]{1,2,0:T(8,128)(2,1)}, s32[2,128]{1,0:T(2,128)S(1)}, s32[2,256]{1,0:T(2,128)S(1)}, /*index=5*/bf16[128,128,256]{2,1,0:T(8,128)(2,1)}, s32[]{:T(128)}) while((s32[]{:T(128)}, f32[2,128,2048]{2,1,0:T(8,128)}, bf16[2,256,2048]{1,2,0:T(8,128)(2,1)}, ...), condition=%wide.region_3.4_spmd, body=%wide.region_2.3_spmd.sunk | while | flops 138477568 | bytes 16913496 | solution.py:82
  605.8 5.7 fusion.84
  614.3 5.7 fusion.84
  621.5 21.3 %multiply_add_fusion = f32[384,2,2048]{2,0,1:T(8,128)S(1)} fusion(bf16[256,2,2048]{2,0,1:T(8,128)(2,1)} %slice.413, bf16[136,2,2048]{2,0,1:T(8,128)(2,1)} %collective-permute-done.17, f32[384]{0:T(512)S(1)} %get-tuple-element.172, f32[2,2048]{1,0:T(2,128)S(1)} %get-tuple-element.146, f32[384]{0:T(512)S(1)} %get-tuple-element.173, ...), kind=kLoop, calls=%fused_computation.33 | loop fusion | flops 73924608 | bytes 9626624 | tf_op jit(solution)/shard_map/add | solution.py:25
  654.6 16.9 %while.20 = (s32[]{:T(128)}, f32[2,128,2048]{2,1,0:T(8,128)}, bf16[2,256,2048]{1,2,0:T(8,128)(2,1)}, s32[2,128]{1,0:T(2,128)S(1)}, s32[2,256]{1,0:T(2,128)S(1)}, /*index=5*/bf16[128,128,256]{2,1,0:T(8,128)(2,1)}, s32[]{:T(128)}) while((s32[]{:T(128)}, f32[2,128,2048]{2,1,0:T(8,128)}, bf16[2,256,2048]{1,2,0:T(8,128)(2,1)}, ...), condition=%wide.region_1.2_spmd, body=%wide.region_0.1_spmd.sunk | while | flops 138477568 | bytes 16913496 | solution.py:82
  656.0 5.7 fusion.80
  664.5 5.7 fusion.80
  671.6 4.2 fusion.42
  683.5 31.3 %fusion.14 = bf16[256,4096]{1,0:T(8,128)(2,1)} fusion(bf16[3,4096,2048]{2,1,0:T(8,128)(2,1)} %constant_dynamic-update-slice_fusion.2, bf16[264,3,2048]{2,0,1:T(8,128)(2,1)} %pad_maximum_fusion, f32[256]{0:T(256)S(1)} %copy-done.27, f32[3,2048]{1,0:T(4,128)S(1)} %get-tuple-element.187, f32[256]{0:T(256)S(1)} %copy-done.28, ...), kind=kOutput, calls=%fused_computation.35 | convolution fusion | flops 12931563520 | bytes 74627072 | tf_op jit(solution)/shard_map/sjc,jdc->sd/dot_general | solution.py:157
  714.8 45.5 %reduce-scatter.2.cloned.1.call-done = bf16[256,2048]{1,0:T(8,128)(2,1)} async-done(((bf16[256,4096]{1,0:T(8,128)(2,1)}), bf16[256,2048]{1,0:T(8,128)(2,1)}) %reduce-scatter.2.cloned.1.call-update) | async-done | bytes 1048592 | tf_op jit(solution)/shard_map/reduce_scatter | solution.py:158
  (184 shorter events, 108.9 us)
Async XLA Ops:
  7.2 353.0 %copy-start = (bf16[128,128]{1,0:T(8,128)(2,1)S(1)}, bf16[128,128]{1,0:T(8,128)(2,1)}, u32[]{:S(2)}) copy-start(bf16[128,128]{1,0:T(8,128)(2,1)} %param.13) | copy-start | bytes 98308
  7.2 524.6 %all-gather.2.cloned.1.call-start = ((), (), s32[]{:S(2)}) async-start(), calls=%async_computation.1 | async-start | bytes 3145728 | tf_op jit(solution)/shard_map/all_gather | solution.py:91
  7.2 40.8 %collective-permute-start = (bf16[3,256,2048]{2,1,0:T(8,128)(2,1)}, bf16[3,256,2048]{2,1,0:T(8,128)(2,1)S(1)}, u32[]{:S(2)}, u32[]{:S(2)}) collective-permute-start(bf16[3,256,2048]{2,1,0:T(8,128)(2,1)} %param.11), channel_id=1, source_target_pairs={{0,2},{2,4},{4,6},{6,8},{8,10},{10,12},{12,14},{14,16},{16,18},{18... | collective-permute-start | bytes 9437192 | tf_op jit(solution)/shard_map/ppermute | solution.py:103
  7.7 70.9 %collective-permute-start.1 = (bf16[3,256,2048]{2,1,0:T(8,128)(2,1)}, bf16[3,256,2048]{2,1,0:T(8,128)(2,1)S(1)}, u32[]{:S(2)}, u32[]{:S(2)}) collective-permute-start(bf16[3,256,2048]{2,1,0:T(8,128)(2,1)} %param.11), channel_id=1, source_target_pairs={{0,30},{2,0},{4,2},{6,4},{8,6},{10,8},{12,10},{14,12},{16,14},{18,... | collective-permute-start | bytes 9437192 | tf_op jit(solution)/shard_map/ppermute | solution.py:106
  48.0 39.5 %collective-permute-start.2 = (bf16[3,256,2048]{2,1,0:T(8,128)(2,1)S(1)}, bf16[3,256,2048]{2,1,0:T(8,128)(2,1)S(1)}, u32[]{:S(2)}, u32[]{:S(2)}) collective-permute-start(bf16[3,256,2048]{2,1,0:T(8,128)(2,1)S(1)} %collective-permute-done), channel_id=1, source_target_pairs={{0,2},{2,4},{4,6},{6,8},{8,10},{10,12},{12,14},{14,16},{16,18},{18... | collective-permute-start | bytes 9437192 | tf_op jit(solution)/shard_map/ppermute | solution.py:103
  78.6 145.5 %copy-start.13 = (bf16[3,256,2048]{2,1,0:T(8,128)(2,1)}, bf16[3,256,2048]{2,1,0:T(8,128)(2,1)S(1)}, u32[]{:S(2)}) copy-start(bf16[3,256,2048]{2,1,0:T(8,128)(2,1)S(1)} %collective-permute-done.1) | copy-start | bytes 9437188
  78.6 69.6 %collective-permute-start.3 = (bf16[3,256,2048]{2,1,0:T(8,128)(2,1)S(1)}, bf16[3,256,2048]{2,1,0:T(8,128)(2,1)S(1)}, u32[]{:S(2)}, u32[]{:S(2)}) collective-permute-start(bf16[3,256,2048]{2,1,0:T(8,128)(2,1)S(1)} %collective-permute-done.1), channel_id=1, source_target_pairs={{0,30},{2,0},{4,2},{6,4},{8,6},{10,8},{12,10},{14,12},{16,14},{18,... | collective-permute-start | bytes 9437192 | tf_op jit(solution)/shard_map/ppermute | solution.py:106
  87.5 136.6 %copy-start.10 = (bf16[3,256,2048]{2,1,0:T(8,128)(2,1)}, bf16[3,256,2048]{2,1,0:T(8,128)(2,1)S(1)}, u32[]{:S(2)}) copy-start(bf16[3,256,2048]{2,1,0:T(8,128)(2,1)S(1)} %collective-permute-done.2) | copy-start | bytes 9437188
  87.5 66.0 %collective-permute-start.4 = (bf16[3,256,2048]{2,1,0:T(8,128)(2,1)S(1)}, bf16[3,256,2048]{2,1,0:T(8,128)(2,1)S(1)}, u32[]{:S(2)}, u32[]{:S(2)}) collective-permute-start(bf16[3,256,2048]{2,1,0:T(8,128)(2,1)S(1)} %collective-permute-done.2), channel_id=1, source_target_pairs={{0,2},{2,4},{4,6},{6,8},{8,10},{10,12},{12,14},{14,16},{16,18},{18... | collective-permute-start | bytes 9437192 | tf_op jit(solution)/shard_map/ppermute | solution.py:103
  149.9 68.8 %collective-permute-start.5 = (bf16[3,256,2048]{2,1,0:T(8,128)(2,1)S(1)}, bf16[3,256,2048]{2,1,0:T(8,128)(2,1)}, u32[]{:S(2)}, u32[]{:S(2)}) collective-permute-start(bf16[3,256,2048]{2,1,0:T(8,128)(2,1)S(1)} %collective-permute-done.3), channel_id=1, source_target_pairs={{0,30},{2,0},{4,2},{6,4},{8,6},{10,8},{12,10},{14,12},{16,14},{18,... | collective-permute-start | bytes 9437192 | tf_op jit(solution)/shard_map/ppermute | solution.py:106
  153.5 65.1 %copy-start.8 = (bf16[3,256,2048]{2,1,0:T(8,128)(2,1)}, bf16[3,256,2048]{2,1,0:T(8,128)(2,1)S(1)}, u32[]{:S(2)}) copy-start(bf16[3,256,2048]{2,1,0:T(8,128)(2,1)S(1)} %collective-permute-done.4) | copy-start | bytes 9437188
  153.5 70.5 %collective-permute-start.6 = (bf16[3,256,2048]{2,1,0:T(8,128)(2,1)S(1)}, bf16[3,256,2048]{2,1,0:T(8,128)(2,1)}, u32[]{:S(2)}, u32[]{:S(2)}) collective-permute-start(bf16[3,256,2048]{2,1,0:T(8,128)(2,1)S(1)} %collective-permute-done.4), channel_id=1, source_target_pairs={{0,2},{2,4},{4,6},{6,8},{8,10},{10,12},{12,14},{14,16},{16,18},{18... | collective-permute-start | bytes 9437192 | tf_op jit(solution)/shard_map/ppermute | solution.py:103
  218.6 81.1 %collective-permute-start.7 = (bf16[3,256,2048]{2,1,0:T(8,128)(2,1)}, bf16[3,256,2048]{2,1,0:T(8,128)(2,1)}, u32[]{:S(2)}, u32[]{:S(2)}) collective-permute-start(bf16[3,256,2048]{2,1,0:T(8,128)(2,1)} %collective-permute-done.5), channel_id=1, source_target_pairs={{0,30},{2,0},{4,2},{6,4},{8,6},{10,8},{12,10},{14,12},{16,14},{18,... | collective-permute-start | bytes 9437192 | tf_op jit(solution)/shard_map/ppermute | solution.py:106
  224.1 77.9 %collective-permute-start.8 = (bf16[3,256,2048]{2,1,0:T(8,128)(2,1)}, bf16[3,256,2048]{2,1,0:T(8,128)(2,1)}, u32[]{:S(2)}, u32[]{:S(2)}) collective-permute-start(bf16[3,256,2048]{2,1,0:T(8,128)(2,1)} %collective-permute-done.6), channel_id=1, source_target_pairs={{0,2},{2,4},{4,6},{6,8},{8,10},{10,12},{12,14},{14,16},{16,18},{18... | collective-permute-start | bytes 9437192 | tf_op jit(solution)/shard_map/ppermute | solution.py:103
  288.5 471.8 %reduce-scatter.2.cloned.1.call-start = ((), (), s32[]{:S(2)}) async-start(), calls=%async_computation.2 | async-start | bytes 3145728 | tf_op jit(solution)/shard_map/reduce_scatter | solution.py:158
  289.9 186.4 %collective-permute-start.16 = (s32[136]{0:T(256)}, s32[136]{0:T(256)}, u32[]{:S(2)}, u32[]{:S(2)}) collective-permute-start(s32[136]{0:T(256)} %slice.310), channel_id=1, source_target_pairs={{0,2},{2,4},{4,6},{6,8},{8,10},{10,12},{12,14},{14,16},{16,18},{18... | collective-permute-start | bytes 1640 | tf_op jit(solution)/shard_map/ppermute | solution.py:10
  296.2 179.3 %collective-permute-start.19 = (s32[128]{0:T(128)}, s32[128]{0:T(128)}, u32[]{:S(2)}, u32[]{:S(2)}) collective-permute-start(s32[128]{0:T(128)} %slice.367), channel_id=1, source_target_pairs={{2,0},{4,2},{6,4},{8,6},{10,8},{12,10},{14,12},{16,14},{18,16},{20... | collective-permute-start | bytes 1544 | tf_op jit(solution)/shard_map/ppermute | solution.py:10
  299.7 69.7 %collective-permute-start.9 = (bf16[3,256,2048]{2,1,0:T(8,128)(2,1)}, bf16[3,256,2048]{2,1,0:T(8,128)(2,1)}, u32[]{:S(2)}, u32[]{:S(2)}) collective-permute-start(bf16[3,256,2048]{2,1,0:T(8,128)(2,1)} %collective-permute-done.7), channel_id=1, source_target_pairs={{0,30},{2,0},{4,2},{6,4},{8,6},{10,8},{12,10},{14,12},{16,14},{18,... | collective-permute-start | bytes 9437192 | tf_op jit(solution)/shard_map/ppermute | solution.py:106
  302.0 68.1 %collective-permute-start.10 = (bf16[3,256,2048]{2,1,0:T(8,128)(2,1)}, bf16[3,256,2048]{2,1,0:T(8,128)(2,1)}, u32[]{:S(2)}, u32[]{:S(2)}) collective-permute-start(bf16[3,256,2048]{2,1,0:T(8,128)(2,1)} %collective-permute-done.8), channel_id=1, source_target_pairs={{0,2},{2,4},{4,6},{6,8},{8,10},{10,12},{12,14},{14,16},{16,18},{18... | collective-permute-start | bytes 9437192 | tf_op jit(solution)/shard_map/ppermute | solution.py:103
  369.4 115.6 %collective-permute-start.11 = (bf16[3,256,2048]{2,1,0:T(8,128)(2,1)}, bf16[3,256,2048]{2,1,0:T(8,128)(2,1)}, u32[]{:S(2)}, u32[]{:S(2)}) collective-permute-start(bf16[3,256,2048]{2,1,0:T(8,128)(2,1)} %collective-permute-done.9), channel_id=1, source_target_pairs={{0,30},{2,0},{4,2},{6,4},{8,6},{10,8},{12,10},{14,12},{16,14},{18,... | collective-permute-start | bytes 9437192 | tf_op jit(solution)/shard_map/ppermute | solution.py:106
  370.1 76.0 %copy-start.5 = (bf16[3,256,2048]{2,1,0:T(8,128)(2,1)S(1)}, bf16[3,256,2048]{2,1,0:T(8,128)(2,1)}, u32[]{:S(2)}) copy-start(bf16[3,256,2048]{2,1,0:T(8,128)(2,1)} %param.11) | copy-start | bytes 9437188
  370.1 118.0 %collective-permute-start.12 = (bf16[3,256,2048]{2,1,0:T(8,128)(2,1)}, bf16[3,256,2048]{2,1,0:T(8,128)(2,1)}, u32[]{:S(2)}, u32[]{:S(2)}) collective-permute-start(bf16[3,256,2048]{2,1,0:T(8,128)(2,1)} %collective-permute-done.10), channel_id=1, source_target_pairs={{0,2},{2,4},{4,6},{6,8},{8,10},{10,12},{12,14},{14,16},{16,18},{18... | collective-permute-start | bytes 9437192 | tf_op jit(solution)/shard_map/ppermute | solution.py:103
  485.0 42.3 %collective-permute-start.13 = (bf16[3,256,2048]{2,1,0:T(8,128)(2,1)}, bf16[3,256,2048]{2,1,0:T(8,128)(2,1)S(1)}, u32[]{:S(2)}, u32[]{:S(2)}) collective-permute-start(bf16[3,256,2048]{2,1,0:T(8,128)(2,1)} %collective-permute-done.11), channel_id=1, source_target_pairs={{0,30},{2,0},{4,2},{6,4},{8,6},{10,8},{12,10},{14,12},{16,14},{18,... | collective-permute-start | bytes 9437192 | tf_op jit(solution)/shard_map/ppermute | solution.py:106
  488.1 41.4 %collective-permute-start.14 = (bf16[3,256,2048]{2,1,0:T(8,128)(2,1)}, bf16[3,256,2048]{2,1,0:T(8,128)(2,1)S(1)}, u32[]{:S(2)}, u32[]{:S(2)}) collective-permute-start(bf16[3,256,2048]{2,1,0:T(8,128)(2,1)} %collective-permute-done.12), channel_id=1, source_target_pairs={{0,2},{2,4},{4,6},{6,8},{8,10},{10,12},{12,14},{14,16},{16,18},{18... | collective-permute-start | bytes 9437192 | tf_op jit(solution)/shard_map/ppermute | solution.py:103
  531.7 54.9 %copy-start.19 = (f32[2048,1]{0,1:T(1,128)S(1)}, f32[2048,1]{0,1:T(1,128)}, u32[]{:S(2)}) copy-start(f32[2048,1]{0,1:T(1,128)} %get-tuple-element.156) | copy-start | bytes 24580
  531.7 54.9 %copy-start.20 = (f32[2048,1]{0,1:T(1,128)S(1)}, f32[2048,1]{0,1:T(1,128)}, u32[]{:S(2)}) copy-start(f32[2048,1]{0,1:T(1,128)} %get-tuple-element.157) | copy-start | bytes 24580
  531.7 54.9 %copy-start.21 = (f32[2048,1]{0,1:T(1,128)S(1)}, f32[2048,1]{0,1:T(1,128)}, u32[]{:S(2)}) copy-start(f32[2048,1]{0,1:T(1,128)} %get-tuple-element.158) | copy-start | bytes 24580
  553.1 33.5 %collective-permute-start.15 = (bf16[8,2048]{1,0:T(8,128)(2,1)S(1)}, bf16[8,2048]{1,0:T(8,128)(2,1)S(1)}, u32[]{:S(2)}, u32[]{:S(2)}) collective-permute-start(bf16[8,2048]{1,0:T(8,128)(2,1)S(1)} %slice_bitcast_fusion.1), channel_id=1, source_target_pairs={{0,2},{2,4},{4,6},{6,8},{8,10},{10,12},{12,14},{14,16},{16,18},{18... | collective-permute-start | bytes 98312 | tf_op jit(solution)/shard_map/ppermute | solution.py:10
  590.7 8.7 %collective-permute-start.18 = (bf16[128,2048]{1,0:T(8,128)(2,1)S(1)}, bf16[128,2048]{1,0:T(8,128)(2,1)}, u32[]{:S(2)}, u32[]{:S(2)}) collective-permute-start(bf16[128,2048]{1,0:T(8,128)(2,1)S(1)} %slice.437), channel_id=1, source_target_pairs={{2,0},{4,2},{6,4},{8,6},{10,8},{12,10},{14,12},{16,14},{18,16},{20... | collective-permute-start | bytes 1572872 | tf_op jit(solution)/shard_map/ppermute | solution.py:10
  594.7 26.8 %collective-permute-start.17 = (bf16[136,2,2048]{2,0,1:T(8,128)(2,1)}, bf16[136,2,2048]{2,0,1:T(8,128)(2,1)}, u32[]{:S(2)}, u32[]{:S(2)}) collective-permute-start(bf16[136,2,2048]{2,0,1:T(8,128)(2,1)} %slice.412), channel_id=1, source_target_pairs={{0,2},{2,4},{4,6},{6,8},{8,10},{10,12},{12,14},{14,16},{16,18},{18... | collective-permute-start | bytes 3342344 | tf_op jit(solution)/shard_map/ppermute | solution.py:10
  676.2 5.3 collective-permute-start.20
  683.5 76.9 %copy-start.1 = (bf16[128,128]{1,0:T(8,128)(2,1)S(1)}, bf16[128,128]{1,0:T(8,128)(2,1)}, u32[]{:S(2)}) copy-start(bf16[128,128]{1,0:T(8,128)(2,1)} %param.13) | copy-start | bytes 98308
  (20 other events, 303.6 us)
Sparse Core Ops, SparseCore 0:
  288.6 34.3 all-gather.1
  714.9 45.3 reduce-scatter.1
